TPU v7x, 32 devices: a whole 2x2x4 slice. The times are simulated.
32 devices in a mesh: seq: 8 (over z, y), tp: 4 (over x, core).
Axes of the slice: x: 2, y: 2, z: 4, core: 2. Of those that a mesh axis runs over, the one named last changes fastest.
Arguments:
- tokens: bfloat16 [2048, 2048], P('seq', 'tp'), may hold values from -6 to 6
- norm_gain: float32 [2048], replicated, may hold values from 0.1 to 1.9
- w_query: bfloat16 [2048, 1024], P(None, 'tp'), may hold values from -0.125 to 0.125
- w_key: bfloat16 [2048, 1024], P(None, 'tp'), may hold values from -0.125 to 0.125
- w_value: bfloat16 [2048, 2048], P(None, 'tp'), may hold values from -0.125 to 0.125
- w_gate_out: bfloat16 [2048, 2048], P(None, 'tp'), may hold values from -0.125 to 0.125
- gate_down: bfloat16 [2048, 16], replicated, may hold values from -0.09272438 to 0.09272438
- gate_up: bfloat16 [16, 1024], P(None, 'tp'), may hold values from -1 to 1.2625
- gate_bias: float32 [1024], P('tp'), may hold values from 1 to 8
- head_gain: float32 [2048], P('tp'), may hold values from 0.1 to 1.9
- w_out: bfloat16 [2048, 2048], P('tp'), may hold values from -0.125 to 0.125
- request_ids: int32 [2048], P('seq'), may hold values from 0 to 3, as said below
Outputs:
- mixed: bfloat16 [2048, 2048], P('seq', 'tp')
Inputs may be any that keep to these rules, and one draw needn't show every extreme that they name: `request_ids`: request numbers never fall along the tokens; every request of 0 to 3 holds 1 to 1024 tokens; request 0 holds fewer than 256 tokens and request 1 holds exactly 1024.
All inputs are finite; a program needn't handle non-finite values.
Results may differ from a plain program's by a relative error of at most 0.015.
Values may be sent and summed in bfloat16 or wider, within the bound.
A program may use at most 128 MiB of HBM per device.

v0:
```python
import jax
import jax.numpy as jnp
from jax import lax
from jax.sharding import PartitionSpec as P

K = 256
V = 512
C = 64


def from_behind(block, axis, distance):
    devices = range(lax.axis_size(axis))
    route = [(i - distance, i) for i in devices if i - distance in devices]
    return lax.ppermute(block, axis, route)


def entering(shard, axis, combine, identity):
    count, position = (lax.axis_size(axis), lax.axis_index(axis))
    everything = jax.tree.map(lambda part: lax.all_gather(part, axis), shard)
    start = jax.tree.map(
        lambda part, zero: jnp.broadcast_to(jnp.asarray(zero, part.dtype), part.shape),
        shard,
        identity,
    )

    def turn(k, before):
        reached = k < position
        new = combine(before, jax.tree.map(lambda part: part[k], everything))
        return jax.tree.map(lambda a, b: jnp.where(reached, a, b), new, before)

    return lax.fori_loop(0, count, turn, start)


def rms(value, gain):
    return value * lax.rsqrt(jnp.mean(value * value, axis=-1, keepdims=True) + 1e-05) * gain


def group_terms(query, key, value, log_decay_rate, ids, prev):
    cum = jnp.cumsum(log_decay_rate, axis=0)
    query_decayed = (query.astype(jnp.float32) * jnp.exp(cum) * K ** (-0.5)).astype(jnp.bfloat16)
    kinv = (key.astype(jnp.float32) * jnp.exp(-cum)).astype(jnp.bfloat16)
    scores = jnp.dot(query_decayed, kinv.T, preferred_element_type=jnp.float32)
    place = jnp.arange(query.shape[0], dtype=jnp.int32)
    allowed = (place[None, :] <= place[:, None]) & (ids[None, :] == ids[:, None])
    weights = jnp.where(allowed, scores, 0.0).astype(jnp.bfloat16)
    intra = jnp.dot(weights, value, preferred_element_type=jnp.float32)
    causal_mask = ids == prev
    keep = (ids == ids[-1]).astype(jnp.float32)[:, None]
    kend = (key.astype(jnp.float32) * jnp.exp(cum[-1:] - cum) * keep).astype(jnp.bfloat16)
    fresh = jnp.dot(kend.T, value, preferred_element_type=jnp.float32)
    decay = jnp.exp(cum[-1]) * (ids[-1] == prev).astype(jnp.float32)
    return (query_decayed, intra, causal_mask, fresh, decay)


def local_pass(query, key, value, log_decay_rate, request_id_block, prev_device):

    def step(carry, item):
        state, product, prev = carry
        qc, kc, vc, gc, sc = item
        query_decayed, intra, causal_mask, fresh, decay = group_terms(qc, kc, vc, gc, sc, prev)
        return (
            (decay[:, None] * state + fresh, decay * product, sc[-1]),
            (query_decayed, intra, causal_mask, state, product),
        )

    start = (jnp.zeros((K, V), jnp.float32), jnp.ones((K,), jnp.float32), prev_device)
    (state, product, _), stacked = lax.scan(
        step, start, (query, key, value, log_decay_rate, request_id_block)
    )
    return (state, product, stacked)


def merge_results(earlier, later):
    return (earlier[0] * later[0], later[0][..., None] * earlier[1] + later[1])


def per_device(
    tokens,
    norm_gain,
    w_query,
    w_key,
    w_value,
    w_gate_out,
    gate_down,
    gate_up,
    gate_bias,
    head_gain,
    w_out,
    request_ids,
):
    whole = lax.all_gather(tokens, "tp", axis=1, tiled=True)
    rows = whole.shape[0]
    blocks = rows // C
    heads = w_value.shape[1] // V
    normed = rms(whole.astype(jnp.float32), norm_gain).astype(jnp.bfloat16)
    low = jnp.dot(normed, gate_down, preferred_element_type=jnp.float32).astype(jnp.bfloat16)
    log_decay_rate = (
        jax.nn.log_sigmoid(jnp.dot(low, gate_up, preferred_element_type=jnp.float32) + gate_bias)
        / 16.0
    )
    query = jnp.dot(normed, w_query, preferred_element_type=jnp.float32).astype(jnp.bfloat16)
    key = jnp.dot(normed, w_key, preferred_element_type=jnp.float32).astype(jnp.bfloat16)
    value = jnp.dot(normed, w_value, preferred_element_type=jnp.float32).astype(jnp.bfloat16)
    opengate = jnp.dot(normed, w_gate_out, preferred_element_type=jnp.float32)
    edge = from_behind(request_ids[-1:] + 1, "seq", 1)
    prev_device = edge[0] - 1
    request_id_block = request_ids.reshape(blocks, C)
    qh = query.reshape(blocks, C, K)
    kh = key.reshape(blocks, C, K)
    vh = value.reshape(blocks, C, V)
    gh = log_decay_rate.reshape(blocks, C, K)
    state, product, stacked = local_pass(qh, kh, vh, gh, request_id_block, prev_device)
    finals = [state]
    products = [product]
    identity = (jnp.ones((heads, K), jnp.float32), jnp.zeros((heads, K, V), jnp.float32))
    _, incoming = entering((jnp.stack(products), jnp.stack(finals)), "seq", merge_results, identity)
    query_decayed, intra, causal_mask, entry, entry_product = stacked
    entry_exact_value = entry + entry_product[:, :, None] * incoming[0][None]
    inter = jnp.einsum(
        "axo,aoe->axe",
        query_decayed.astype(jnp.float32),
        entry_exact_value,
        precision=lax.Precision.HIGHEST,
    )
    attn = (intra + jnp.where(causal_mask[..., None], inter, 0.0)).reshape(rows, V)
    gated = rms(attn, head_gain) * jax.nn.silu(opengate)
    results = gated.astype(jnp.bfloat16)
    partial_out = jnp.dot(results, w_out, preferred_element_type=jnp.float32)
    mixed = lax.psum_scatter(
        partial_out.astype(jnp.bfloat16), "tp", scatter_dimension=1, tiled=True
    )
    return mixed


def solution(mesh):
    return jax.shard_map(
        per_device,
        mesh=mesh,
        in_specs=(
            P("seq", "tp"),
            P(),
            P(None, "tp"),
            P(None, "tp"),
            P(None, "tp"),
            P(None, "tp"),
            P(),
            P(None, "tp"),
            P("tp"),
            P("tp"),
            P("tp", None),
            P("seq"),
        ),
        out_specs=P("seq", "tp"),
        check_vma=False,
    )
```

profile of v0, /device:TPU:26, one launch (start us, length us, event | category | flops | bytes accessed | tf_op | source)
XLA Modules:
  0.0 184.4 jit_solution(17676101719912972837)
XLA Ops:
  6.5 0.7 all-gather.6.cloned.1.call-update
  7.3 1.3 slice.13
  9.2 4.7 %collective-permute-start = (s32[1]{0:T(128)}, s32[1]{0:T(128)}, u32[]{:S(2)}, u32[]{:S(2)}) collective-permute-start(s32[1]{0:T(128)} %add.82), channel_id=1, source_target_pairs={{0,4},{4,8},{8,12},{12,16},{16,20},{20,24},{24,28},{1,5},{5,9},{9,... | collective-permute-start | bytes 20 | tf_op jit(solution)/shard_map/ppermute | solution.py:14
  13.9 0.8 reshape.134
  14.7 1.0 collective-permute-done
  16.3 9.4 %all-gather.6.cloned.1.call-done = bf16[256,2048]{1,0:T(8,128)(2,1)} async-done(((bf16[256,512]{1,0:T(8,128)(2,1)}), bf16[256,2048]{1,0:T(8,128)(2,1)}) %all-gather.6.cloned.1.call-update) | async-done | bytes 1048592 | tf_op jit(solution)/shard_map/all_gather | solution.py:91
  25.7 1.5 fusion.42
  27.3 2.8 %convolution_convert_fusion.1 = bf16[256,512]{1,0:T(8,128)(2,1)S(1)} fusion(bf16[2048,512]{1,0:T(8,128)(2,1)} %param.20, bf16[256,2048]{1,0:T(8,128)(2,1)} %all-gather.6.cloned.1.call-done, f32[2048]{0:T(1024)} %param.17, f32[256]{0:T(256)S(1)} %add_rsqrt_fusion.1), kind=kOutput, calls=%fused_computation.60 | convolution fusion | flops 539099136 | bytes 3417088 | tf_op jit(solution)/shard_map/dot_general | solution.py:103
  30.2 0.5 convolution_convert_fusion.3
  30.7 0.7 copy-done.12
  31.4 0.5 convolution_convert_fusion.2
  31.9 0.3 copy-done.13
  32.2 2.0 %fusion.58 = f32[256,256]{1,0:T(8,128)S(1)} fusion(bf16[16,256]{1,0:T(8,128)(2,1)S(1)} %copy-done.14, bf16[2048,16]{0,1:T(8,128)(2,1)S(1)} %copy-done.13, f32[256]{0:T(256)S(1)} %copy-done.18, bf16[256,2048]{1,0:T(8,128)(2,1)} %all-gather.6.cloned.1.call-done, f32[2048]{0:T(1024)S(1)} %copy-done.15, f32[256]{0:T(256)S(1)} %add_rsqrt_fusion.1), kind=kOutput, calls=%fused_computation.75 | convolution fusion | flops 21630976 | bytes 1394688 | tf_op jit(solution)/shard_map/dot_general | solution.py:98
  34.2 28.6 %while.41 = (s32[]{:T(128)}, f32[256,512]{1,0:T(8,128)S(1)}, f32[256]{0:T(256)S(1)}, s32[]{:T(128)}, bf16[4,64,256]{2,1,0:T(8,128)(2,1)}, /*index=5*/f32[4,64,51...) while((s32[]{:T(128)}, f32[256,512]{1,0:T(8,128)S(1)}, ...), condition=%wide.region_3.4_spmd.clone.clone, body=%wide.region_1.3_spmd.clone.sunk.clone | while | flops 24925124 | bytes 3067847 | solution.py:67
  34.2 0.6 slice.21
  35.4 0.1 reduce_window_sum.17
  35.5 0.6 compare_convert_fusion.3
  36.1 0.8 bitcast_dynamic-update-slice_fusion.3
  37.0 0.3 convolution_add_fusion.4
  37.3 1.3 dynamic_update_slice.42
  38.6 0.9 fusion.103
  39.5 0.6 fusion.102
  40.2 0.6 copy-done.9
  41.4 0.6 slice.21
  42.7 0.6 compare_convert_fusion.3
  43.3 0.8 bitcast_dynamic-update-slice_fusion.3
  44.1 0.3 convolution_add_fusion.4
  44.4 1.3 dynamic_update_slice.42
  45.7 0.9 fusion.103
  46.7 0.6 fusion.102
  47.3 0.6 copy-done.9
  48.5 0.6 slice.21
  49.8 0.6 compare_convert_fusion.3
  50.4 0.8 bitcast_dynamic-update-slice_fusion.3
  51.2 0.3 convolution_add_fusion.4
  51.6 1.3 dynamic_update_slice.42
  52.9 1.0 fusion.103
  53.8 0.6 fusion.102
  54.5 0.6 copy-done.9
  55.7 0.6 slice.21
  57.0 0.6 compare_convert_fusion.3
  57.6 0.8 bitcast_dynamic-update-slice_fusion.3
  58.4 0.3 convolution_add_fusion.4
  58.7 1.3 dynamic_update_slice.42
  60.0 0.9 fusion.103
  61.0 0.6 fusion.102
  61.6 0.6 copy-done.9
  62.8 0.8 copy-done.1
  63.7 16.1 %all-gather.2 = f32[8,1,256]{2,1,0:T(1,128)S(1)} all-gather(f32[1,1,256]{2,1,0:T(1,128)S(1)} %bitcast.158), channel_id=2, replica_groups=mesh['seq'=8,'tp'=4] {'seq'}, dimensions={0}, use_global_device_ids=true | all-gather | bytes 9216 | tf_op jit(solution)/shard_map/all_gather | solution.py:19
  79.8 56.6 %all-gather.8.cloned.1.call-done = f32[2048,512]{1,0:T(8,128)} async-done(((f32[256,512]{1,0:T(8,128)}), f32[2048,512]{1,0:T(8,128)}) %all-gather.8.cloned.1.call-update) | async-done | bytes 4194320 | tf_op jit(solution)/shard_map/all_gather | solution.py:19
  136.4 9.7 %while.42 = (s32[]{:T(128)}, f32[1,256,512]{2,1,0:T(8,128)S(1)}, s32[]{:T(128)}, f32[8,1,256]{2,1,0:T(1,128)S(1)}, f32[8,1,256,512]{3,2,1,0:T(8,128)}) while((s32[]{:T(128)}, f32[1,256,512]{2,1,0:T(8,128)S(1)}, s32[]{:T(128)}, f32[8,1,256]{2,1,0:T(1,128)S(1)}, f32[8,1,256,512]{3,2,1,0:T(8,128)}) %tuple.77), condition=%wide.region_5.6_spmd.clone.clone, body=%wide.region_4.5_spmd.clone.sunk.clone | while | flops 524292 | bytes 1576025 | solution.py:31
  136.4 1.2 fusion.104
  137.6 1.2 fusion.104
  138.9 1.2 fusion.104
  140.1 1.2 fusion.104
  141.3 1.2 fusion.104
  142.5 1.2 fusion.104
  143.7 1.2 fusion.104
  144.9 1.2 fusion.104
  146.2 2.7 %fusion.48 = f32[4,64,512]{2,1,0:T(8,128)S(1)} fusion(bf16[4,64,256]{2,1,0:T(8,128)(2,1)S(1)} %copy-done.4, f32[4,256,512]{2,1,0:T(8,128)} %get-tuple-element.180, f32[256,512]{1,0:T(8,128)S(1)} %bitcast.147, f32[4,256]{1,0:T(4,128)S(1)} %copy-done.5, pred[4,64]{1,0:T(4,128)(4,1)S(1)} %copy-done.10), kind=kOutput, calls=%fused_computation.59 | convolution fusion | flops 403832832 | bytes 3281152 | tf_op jit(solution)/shard_map/axo,aoe->axe/dot_general | solution.py:119
  148.9 0.1 multiply_reduce_fusion
  149.2 2.8 %fusion.56 = bf16[256,512]{1,0:T(8,128)(2,1)S(1)} fusion(f32[4,64,512]{2,1,0:T(8,128)S(1)} %get-tuple-element.292, f32[512]{0:T(512)S(1)} %copy-done.17, f32[256]{0:T(256)S(1)} %rsqrt.21, bf16[2048,512]{1,0:T(8,128)(2,1)} %param.21, bf16[256,2048]{1,0:T(8,128)(2,1)} %all-gather.6.cloned.1.call-done, f32[2048]{0:T(1024)S(1)} %copy-done.16, f32[256]{0:T(256)S(1)} %copy-done.7), kind=kOutput, calls=%fused_computation.72 | convolution fusion | flops 540016640 | bytes 3944448 | tf_op jit(solution)/shard_map/dot_general | solution.py:104
  152.0 1.8 convolution_convert_fusion
  153.8 24.1 %reduce-scatter.2.cloned.1.call-done = bf16[256,512]{1,0:T(8,128)(2,1)} async-done(((bf16[256,2048]{1,0:T(8,128)(2,1)}), bf16[256,512]{1,0:T(8,128)(2,1)}) %reduce-scatter.2.cloned.1.call-update) | async-done | bytes 262160 | tf_op jit(solution)/shard_map/reduce_scatter | solution.py:129
  (90 shorter events, 1.0 us)
Async XLA Ops:
  6.5 145.4 %copy-start = (bf16[512,2048]{1,0:T(8,128)(2,1)S(1)}, bf16[512,2048]{1,0:T(8,128)(2,1)}, u32[]{:S(2)}) copy-start(bf16[512,2048]{1,0:T(8,128)(2,1)} %param.26) | copy-start | bytes 6291460
  6.5 19.2 %all-gather.6.cloned.1.call-start = ((), (), s32[]{:S(2)}) async-start(), calls=%async_computation.1 | async-start | bytes 1310720 | tf_op jit(solution)/shard_map/all_gather | solution.py:91
  7.3 129.1 %all-gather.8.cloned.1.call-start = ((), (), s32[]{:S(2)}) async-start(), calls=%async_computation.3 | async-start | bytes 4718592 | tf_op jit(solution)/shard_map/all_gather | solution.py:19
  9.2 6.4 %collective-permute-start = (s32[1]{0:T(128)}, s32[1]{0:T(128)}, u32[]{:S(2)}, u32[]{:S(2)}) collective-permute-start(s32[1]{0:T(128)} %add.82), channel_id=1, source_target_pairs={{0,4},{4,8},{8,12},{12,16},{16,20},{20,24},{24,28},{1,5},{5,9},{9,... | collective-permute-start | bytes 20 | tf_op jit(solution)/shard_map/ppermute | solution.py:14
  27.2 4.6 %copy-start.6 = (f32[256]{0:T(256)}, f32[256]{0:T(256)S(1)}, u32[]{:S(2)}) copy-start(f32[256]{0:T(256)S(1)} %add_rsqrt_fusion.1) | copy-start | bytes 3076
  27.3 2.9 %copy-start.2 = (bf16[256,2048]{1,0:T(8,128)(2,1)S(1)}, bf16[256,2048]{1,0:T(8,128)(2,1)}, u32[]{:S(2)}) copy-start(bf16[256,2048]{1,0:T(8,128)(2,1)} %all-gather.6.cloned.1.call-done) | copy-start | bytes 3145732
  27.3 2.9 %copy-start.11 = (bf16[2048,256]{1,0:T(8,128)(2,1)S(1)}, bf16[2048,256]{1,0:T(8,128)(2,1)}, u32[]{:S(2)}) copy-start(bf16[2048,256]{1,0:T(8,128)(2,1)} %param.19) | copy-start | bytes 3145732
  27.3 2.9 %copy-start.15 = (f32[2048]{0:T(1024)S(1)}, f32[2048]{0:T(1024)}, u32[]{:S(2)}) copy-start(f32[2048]{0:T(1024)} %param.17) | copy-start | bytes 24580
  30.2 1.2 copy-start.12
  31.4 0.8 copy-start.13
  31.4 0.8 copy-start.14
  31.4 0.8 copy-start.18
  35.5 4.7 %copy-start.8 = (pred[4,64]{1,0:T(4,128)(4,1)S(1)}, pred[4,64]{1,0:T(4,128)(4,1)}, u32[]{:S(2)}) copy-start(pred[4,64]{1,0:T(4,128)(4,1)} %get-tuple-element.489) | copy-start | bytes 772 | tf_op jit(solution)/shard_map/while
  40.2 0.6 copy-start.9
  42.6 4.7 %copy-start.8 = (pred[4,64]{1,0:T(4,128)(4,1)S(1)}, pred[4,64]{1,0:T(4,128)(4,1)}, u32[]{:S(2)}) copy-start(pred[4,64]{1,0:T(4,128)(4,1)} %get-tuple-element.489) | copy-start | bytes 772 | tf_op jit(solution)/shard_map/while
  47.3 0.6 copy-start.9
  49.8 4.7 %copy-start.8 = (pred[4,64]{1,0:T(4,128)(4,1)S(1)}, pred[4,64]{1,0:T(4,128)(4,1)}, u32[]{:S(2)}) copy-start(pred[4,64]{1,0:T(4,128)(4,1)} %get-tuple-element.489) | copy-start | bytes 772 | tf_op jit(solution)/shard_map/while
  54.5 0.6 copy-start.9
  56.9 4.7 %copy-start.8 = (pred[4,64]{1,0:T(4,128)(4,1)S(1)}, pred[4,64]{1,0:T(4,128)(4,1)}, u32[]{:S(2)}) copy-start(pred[4,64]{1,0:T(4,128)(4,1)} %get-tuple-element.489) | copy-start | bytes 772 | tf_op jit(solution)/shard_map/while
  61.6 0.6 copy-start.9
  62.8 0.8 copy-start.1
  63.7 114.2 %reduce-scatter.2.cloned.1.call-start = ((), (), s32[]{:S(2)}) async-start(), calls=%async_computation.2 | async-start | bytes 1310720 | tf_op jit(solution)/shard_map/reduce_scatter | solution.py:129
  136.4 9.7 %copy-start.4 = (bf16[4,64,256]{2,1,0:T(8,128)(2,1)S(1)}, bf16[4,64,256]{2,1,0:T(8,128)(2,1)}, u32[]{:S(2)}) copy-start(bf16[4,64,256]{2,1,0:T(8,128)(2,1)} %get-tuple-element.179) | copy-start | bytes 393220
  136.4 9.8 %copy-start.5 = (f32[4,256]{1,0:T(4,128)S(1)}, f32[4,256]{1,0:T(4,128)}, u32[]{:S(2)}) copy-start(f32[4,256]{1,0:T(4,128)} %get-tuple-element.181) | copy-start | bytes 12292
  136.4 9.8 %copy-start.10 = (pred[4,64]{1,0:T(4,128)(4,1)S(1)}, pred[4,64]{1,0:T(4,128)(4,1)}, u32[]{:S(2)}) copy-start(pred[4,64]{1,0:T(4,128)(4,1)} %get-tuple-element.178) | copy-start | bytes 772
  146.1 2.8 %copy-start.3 = (f32[4,64,512]{2,1,0:T(8,128)S(1)}, f32[4,64,512]{2,1,0:T(8,128)}, u32[]{:S(2)}) copy-start(f32[4,64,512]{2,1,0:T(8,128)} %get-tuple-element.177) | copy-start | bytes 1572868
  146.2 3.0 %copy-start.7 = (f32[256]{0:T(256)S(1)}, f32[256]{0:T(256)}, u32[]{:S(2)}) copy-start(f32[256]{0:T(256)} %copy-done.6) | copy-start | bytes 3076
  146.2 3.0 %copy-start.16 = (f32[2048]{0:T(1024)S(1)}, f32[2048]{0:T(1024)}, u32[]{:S(2)}) copy-start(f32[2048]{0:T(1024)} %param.17) | copy-start | bytes 24580
  146.2 3.0 %copy-start.17 = (f32[512]{0:T(512)S(1)}, f32[512]{0:T(512)}, u32[]{:S(2)}) copy-start(f32[512]{0:T(512)} %param.25) | copy-start | bytes 6148
Sparse Core Ops, SparseCore 0:
  8.9 16.7 all-gather.5
  63.8 72.5 all-gather.7
  153.9 23.9 reduce-scatter.1
where the time goes:
time: 188 us; the launch traced here: 184 us
  waiting for transfers between devices  91.8 us (49%)
  other arithmetic  19.8 us (11%)
  matrix products  18.1 us (10%)
  blocking collectives  16.1 us (9%)
  between operations  14.6 us (8%)
  local copies, waits for them, and re-layouts  14.1 us (8%)
  loops' own time  5.09 us (3%)
  starting transfers between devices  4.79 us (3%)
    all_gather x1, waiting for transfers between devices, entering(): everything = jax.tree.map(lambda part: lax.all_gather(part, axis), shard)  56.6 us
    reduce_scatter x1, waiting for transfers between devices, per_device(): lax.psum_scatter(partial_out.astype(jnp.bfloat16), 'tp', scatter_dimensio...  24.1 us
    all_gather x1, blocking collectives, entering(): everything = jax.tree.map(lambda part: lax.all_gather(part, axis), shard)  16.1 us
    select_n x8, other arithmetic, turn(): return jax.tree.map(lambda a, b: jnp.where(reached, a, b), new, before)  9.43 us
    all_gather x1, waiting for transfers between devices, per_device(): whole = lax.all_gather(tokens, 'tp', axis=1, tiled=True)  9.43 us
    dynamic_update_slice x8, other arithmetic, local_pass(): lax.scan(step, start, (query, key, value, log_decay_rate, request_id_block))  5.9 us
    dynamic_update_slice x8, local copies, waits for them, and re-layouts, local_pass(): lax.scan(step, start, (query, key, value, log_decay_rate, request_id_block))  5.34 us
    another operation x1, loops' own time, local_pass(): lax.scan(step, start, (query, key, value, log_decay_rate, request_id_block))  4.85 us
  transfers between devices with their start and end apart: 4, of which 4 were waited for; matrix products, arithmetic and copies ran while one was open for 1% of the time, Pallas kernels for 0%

commit v1 on v0

v1 whole, which is shorter than its diff:
```python
import functools

import jax
import jax.numpy as jnp
from jax import lax
from jax.experimental import pallas as pl
from jax.experimental.pallas import tpu as pltpu
from jax.sharding import PartitionSpec as P

K = 256
V = 512
C = 64
F32 = jnp.float32
BF16 = jnp.bfloat16
MESH = pl.DeviceIdType.MESH
TOKEN_CHUNKS = 4
STATE_CHUNKS = 4
OUT_CHUNKS = 2


def dot(a, b):
    return jnp.dot(a, b, preferred_element_type=F32)


def dot_nt(a, b):
    return lax.dot_general(a, b, (((1,), (1,)), ((), ())), preferred_element_type=F32)


def dot_tn(a, b):
    return lax.dot_general(a, b, (((0,), (0,)), ((), ())), preferred_element_type=F32)


def kernel(
    pairs,
    tokens_ref, gain_ref, wq_hbm, wk_hbm, wv_hbm, wg_hbm, down_ref, up_ref, bias_ref,
    head_gain_ref, wo_hbm, ids_ref,
    out_ref,
    tok, wq, wk, wv, wg, wo,
    acc_q, acc_k, acc_v, acc_g, acc_low, ssq_all,
    attn_ref, qin_ref, gated_ref,
    id_out, id_in, p_own, p_other,
    s_own, s_other, e_in, e_out, i_out, incoming,
    mate_out, mate_in, x_out, x_in, keep_x, keep_own,
    load_sem, tok_sem, tok_x, tok_x_in, tok_mate, tok_mate_in, tok_fwd, tok_fwd_in,
    id_sem, p_sem, s_sem, s_sem_in, e_sem, e_sem_in, i_sem, i_sem_in,
    m_sem, m_sem_in, x_sem, x_sem_in, ssq_sem, ssq_sem_in,
):
    s, t = lax.axis_index("seq"), lax.axis_index("tp")
    y, g = s % 2, s // 2
    rows, feats = tokens_ref.shape
    mate = t + 1 - 2 * (t % 2)
    across = (t + 2) % 4
    diagonal = (mate + 2) % 4
    partner = s + 1 - 2 * y
    last = pairs - 1

    def remote(src, dst, send, recv, where):
        return pltpu.make_async_remote_copy(
            src_ref=src, dst_ref=dst, send_sem=send, recv_sem=recv,
            device_id=where, device_id_type=MESH)

    own_tokens = pltpu.make_async_copy(tokens_ref, tok.at[t], tok_sem)
    own_tokens.start()
    loads = [
        pltpu.make_async_copy(src, dst, load_sem.at[i])
        for i, (src, dst) in enumerate([(wk_hbm, wk), (wv_hbm, wv), (wq_hbm, wq), (wg_hbm, wg)])
    ]
    loads += [
        pltpu.make_async_copy(wo_hbm.at[:, pl.ds(j * feats, feats)], wo.at[j], load_sem.at[4 + j])
        for j in range(4)
    ]
    for load in loads:
        load.start()

    barrier = pltpu.get_barrier_semaphore()
    up_g, down_g = (g + 1) % pairs, (g + last) % pairs
    skew = ((g + y * 2 - 1 + pairs) % pairs) * 2 + 1 - y
    for device in ((s, mate), (s, across), (s, diagonal), (partner, t), (up_g * 2 + y, t), (down_g * 2 + y, t), (skew, t)):
        pl.semaphore_signal(barrier, inc=1, device_id=device, device_id_type=MESH)
    id_row = ids_ref[...].astype(F32)
    id_last = id_row[:, rows - 1:rows]
    id_out[...] = jnp.broadcast_to(id_last, id_out.shape)
    acc_q[...] = jnp.zeros_like(acc_q)
    acc_k[...] = jnp.zeros_like(acc_k)
    acc_v[...] = jnp.zeros_like(acc_v)
    acc_g[...] = jnp.zeros_like(acc_g)
    acc_low[...] = jnp.zeros_like(acc_low)
    own_tokens.wait()
    own = tok[t].astype(F32)
    squares = jnp.sum(own * own, axis=-1, keepdims=True)
    ssq_all[0] = jnp.broadcast_to(squares, (rows, 128)).T[0:8]
    pl.semaphore_wait(barrier, 7)
    send_ssq = [
        remote(ssq_all.at[0], ssq_all.at[i + 1], ssq_sem.at[i], ssq_sem_in.at[i], (s, peer))
        for i, peer in enumerate((mate, across, diagonal))
    ]
    for copy in send_ssq:
        copy.start()

    size = rows // TOKEN_CHUNKS

    def piece(block, c):
        return tok.at[block, pl.ds(c * size, size)]

    to_x = [remote(piece(t, c), piece(t, c), tok_x.at[c], tok_x_in.at[c], (s, across)) for c in range(TOKEN_CHUNKS)]
    to_mate = [remote(piece(t, c), piece(t, c), tok_mate.at[c], tok_mate_in.at[c], (s, mate)) for c in range(TOKEN_CHUNKS)]
    from_x = [remote(piece(across, c), piece(across, c), tok_x.at[c], tok_x_in.at[c], (s, across)) for c in range(TOKEN_CHUNKS)]
    from_mate = [remote(piece(mate, c), piece(mate, c), tok_mate.at[c], tok_mate_in.at[c], (s, mate)) for c in range(TOKEN_CHUNKS)]
    forward = [remote(piece(across, c), piece(across, c), tok_fwd.at[c], tok_fwd_in.at[c], (s, mate)) for c in range(TOKEN_CHUNKS)]
    from_fwd = [remote(piece(diagonal, c), piece(diagonal, c), tok_fwd.at[c], tok_fwd_in.at[c], (s, mate)) for c in range(TOKEN_CHUNKS)]
    for c in range(TOKEN_CHUNKS):
        to_x[c].start()
        to_mate[c].start()

    send_id = remote(id_out, id_in, id_sem.at[0], id_sem.at[1], (s + 1, t))

    @pl.when(s < 2 * pairs - 1)
    def _():
        send_id.start()

    def project(block):
        xg = (tok[block].astype(F32) * r * gain_ref[block]).astype(BF16)
        acc_low[...] += dot_nt(xg, down_ref[:, pl.ds(pl.multiple_of(block * feats, feats), feats)])
        acc_k[...] += dot(xg, wk[block])
        acc_v[...] += dot(xg, wv[block])
        acc_q[...] += dot(xg, wq[block])
        acc_g[...] += dot(xg, wg[block])

    for copy in send_ssq:
        copy.wait_recv()
    total = ssq_all[0] + ssq_all[1] + ssq_all[2] + ssq_all[3]
    scale_row = lax.rsqrt(total / (4 * feats) + 1e-5)[0:1]
    r = jnp.broadcast_to(scale_row, (128, rows)).T[:, 0:1]
    for load in loads[:4]:
        load.wait()
    project(t)
    from_x[0].wait_recv()
    forward[0].start()
    for c in range(TOKEN_CHUNKS):
        from_mate[c].wait_recv()
    project(mate)
    for c in range(1, TOKEN_CHUNKS):
        from_x[c].wait_recv()
        forward[c].start()
    project(across)
    for c in range(TOKEN_CHUNKS):
        from_fwd[c].wait_recv()
    project(diagonal)

    low = acc_low[...].astype(BF16)
    z = dot(low, up_ref[...]) + bias_ref[...]
    rate = (jnp.minimum(z, 0.0) - jnp.log1p(jnp.exp(-jnp.abs(z)))) / 16.0
    row = lax.broadcasted_iota(jnp.int32, (rows, rows), 0)
    col = lax.broadcasted_iota(jnp.int32, (rows, rows), 1)
    within = jnp.where((row // C == col // C) & (col <= row), 1.0, 0.0).astype(BF16)
    high = rate.astype(BF16)
    rest = rate - high.astype(F32)
    middle = rest.astype(BF16)
    tiny = (rest - middle.astype(F32)).astype(BF16)
    cum = dot(within, high) + dot(within, middle) + dot(within, tiny)
    blocks = rows // C
    totals = [cum[(b + 1) * C - 1:(b + 1) * C] for b in range(blocks)]
    id_col = jnp.broadcast_to(id_row, (rows, rows)).T

    @pl.when(s == 0)
    def _():
        id_in[...] = jnp.full_like(id_in, -1.0)

    @pl.when(s > 0)
    def _():
        send_id.wait_recv()

    id_prev = id_in[0:1, 0:1]
    key = acc_k[...].astype(BF16).astype(F32)
    value = acc_v[...].astype(BF16)
    keep = jnp.where(id_col[:, 0:1] == id_last, 1.0, 0.0)
    zero = jnp.zeros_like(totals[0])
    kend, kdev = [], []
    for b in range(blocks):
        mine = slice(b * C, (b + 1) * C)
        end = key[mine] * jnp.exp(totals[b] - cum[mine])
        kend.append(end)
        kdev.append((end * jnp.exp(sum(totals[b + 1:], zero)) * keep[mine]).astype(BF16))
    state = dot_tn(value, jnp.concatenate(kdev, axis=0))
    s_own[...] = state.astype(BF16)
    going_on = jnp.where(id_last == id_prev, 1.0, 0.0)
    p_own[...] = jnp.broadcast_to(jnp.exp(sum(totals, zero)) * going_on, p_own.shape)

    half = V // 2
    span = half // STATE_CHUNKS

    def part(ref, owner, c):
        return ref.at[pl.ds(pl.multiple_of(owner * half + c * span, span), span)]

    def small(ref, c):
        return ref.at[pl.ds(c * span, span)]

    send_p = remote(p_own, p_other, p_sem.at[0], p_sem.at[1], (partner, t))
    send_p.start()
    swap = [remote(part(s_own, 1 - y, c), small(s_other, c), s_sem.at[c], s_sem_in.at[c], (partner, t)) for c in range(STATE_CHUNKS)]
    for c in range(STATE_CHUNKS):
        swap[c].start()
    chain = [remote(small(e_out, c), small(e_in, c), e_sem.at[c], e_sem_in.at[c], (s + 2, t)) for c in range(STATE_CHUNKS)]
    give = [remote(small(i_out, c), part(incoming, y, c), i_sem.at[c], i_sem_in.at[c], (partner, t)) for c in range(STATE_CHUNKS)]
    take = [remote(small(i_out, c), part(incoming, 1 - y, c), i_sem.at[c], i_sem_in.at[c], (partner, t)) for c in range(STATE_CHUNKS)]

    grow = jnp.exp(cum)
    query = acc_q[...].astype(BF16).astype(F32)
    qdec = (query * grow * K ** -0.5).astype(BF16)
    kinv = (key * jnp.exp(-cum)).astype(BF16)
    from_prev = jnp.where(id_col[:, 0:1] == id_prev, 1.0, 0.0)
    for b in range(blocks):
        mine = slice(b * C, (b + 1) * C)
        seen = (b + 1) * C
        keys = [
            (kend[a] * jnp.exp(sum(totals[a + 1:b], zero))).astype(BF16) for a in range(b)
        ] + [kinv[mine]]
        scores = dot_nt(qdec[mine], jnp.concatenate(keys, axis=0))
        allowed = (col[mine, :seen] <= row[mine, :seen]) & (id_col[mine, :seen] == id_row[:, :seen])
        weights = jnp.where(allowed, scores, 0.0).astype(BF16)
        attn_ref[mine, :] = dot(weights, value[:seen])
        qin_ref[mine, :] = (
            qdec[mine].astype(F32) * jnp.exp(sum(totals[:b], zero)) * from_prev[mine]
        ).astype(BF16)

    @pl.when(g == 0)
    def _():
        e_in[...] = jnp.zeros_like(e_in)

    second = y.astype(F32)
    first = 1.0 - second
    send_p.wait_recv()
    own_decay, other_decay = p_own[0:1, :], p_other[0:1, :]
    p0 = own_decay * first + other_decay * second
    p1 = own_decay * second + other_decay * first
    for c in range(STATE_CHUNKS):
        swap[c].wait_recv()
        mine = pl.ds(c * span, span)
        place = pl.ds(pl.multiple_of(y * half + c * span, span), span)
        a, b = s_own[place, :].astype(F32), s_other[mine, :].astype(F32)
        s0 = a * first + b * second
        s1 = a * second + b * first

        @pl.when(g > 0)
        def _():
            chain[c].wait_recv()

        entry = e_in[mine, :].astype(F32)
        middle_state = p0 * entry + s0
        e_out[mine, :] = (p1 * middle_state + s1).astype(BF16)

        @pl.when(g < last)
        def _():
            chain[c].start()

        i_out[mine, :] = (middle_state * first + entry * second).astype(BF16)
        give[c].start()
        incoming[place, :] = (entry * first + middle_state * second).astype(BF16)
    for c in range(STATE_CHUNKS):
        take[c].wait_recv()

    attn = attn_ref[...] + dot_nt(qin_ref[...], incoming[...])
    scale = lax.rsqrt(jnp.mean(attn * attn, axis=-1, keepdims=True) + 1e-5)
    opengate = acc_g[...]
    gated_ref[...] = (attn * scale * head_gain_ref[...] * (opengate * jax.nn.sigmoid(opengate))).astype(BF16)
    for load in loads[4:]:
        load.wait()
    lot = rows // OUT_CHUNKS

    def lines(c):
        return pl.ds(c * lot, lot)

    share = [
        [remote(mate_out.at[k, lines(c)], mate_in.at[k, lines(c)], m_sem.at[k, c], m_sem_in.at[k, c], (s, mate)) for c in range(OUT_CHUNKS)]
        for k in range(2)
    ]
    over = [remote(x_out.at[lines(c)], x_in.at[lines(c)], x_sem.at[c], x_sem_in.at[c], (s, across)) for c in range(OUT_CHUNKS)]
    for c in range(OUT_CHUNKS):
        mate_out[0, lines(c), :] = dot(gated_ref[lines(c), :], wo[diagonal]).astype(BF16)
        share[0][c].start()
        keep_x[lines(c), :] = dot(gated_ref[lines(c), :], wo[across])
    for c in range(OUT_CHUNKS):
        share[0][c].wait_recv()
        x_out[lines(c), :] = (keep_x[lines(c), :] + mate_in[0, lines(c), :].astype(F32)).astype(BF16)
        over[c].start()
    for c in range(OUT_CHUNKS):
        mate_out[1, lines(c), :] = dot(gated_ref[lines(c), :], wo[mate]).astype(BF16)
        share[1][c].start()
        keep_own[lines(c), :] = dot(gated_ref[lines(c), :], wo[t])
    for c in range(OUT_CHUNKS):
        share[1][c].wait_recv()
        over[c].wait_recv()
        out_ref[lines(c), :] = (
            keep_own[lines(c), :] + mate_in[1, lines(c), :].astype(F32) + x_in[lines(c), :].astype(F32)
        ).astype(BF16)

    for copy in to_x + to_mate + forward + send_ssq + [send_p] + swap + give + share[0] + share[1] + over:
        copy.wait_send()

    @pl.when(s < 2 * pairs - 1)
    def _():
        send_id.wait_send()

    @pl.when(g < last)
    def _():
        for c in range(STATE_CHUNKS):
            chain[c].wait_send()


def per_device(
    pairs,
    tokens, norm_gain, w_query, w_key, w_value, w_gate_out, gate_down, gate_up, gate_bias,
    head_gain, w_out, request_ids,
):
    rows, feats = tokens.shape
    ranks = gate_down.shape[1]
    vmem = pl.BlockSpec(memory_space=pltpu.VMEM)
    hbm = pl.BlockSpec(memory_space=pl.ANY)
    half = V // 2
    dma = pltpu.SemaphoreType.DMA
    scratch = [
        pltpu.VMEM((4, rows, feats), BF16),
        pltpu.VMEM((4, feats, K), BF16),
        pltpu.VMEM((4, feats, K), BF16),
        pltpu.VMEM((4, feats, V), BF16),
        pltpu.VMEM((4, feats, V), BF16),
        pltpu.VMEM((4, V, feats), BF16),
        pltpu.VMEM((rows, K), F32),
        pltpu.VMEM((rows, K), F32),
        pltpu.VMEM((rows, V), F32),
        pltpu.VMEM((rows, V), F32),
        pltpu.VMEM((rows, ranks), F32),
        pltpu.VMEM((4, 8, rows), F32),
        pltpu.VMEM((rows, V), F32),
        pltpu.VMEM((rows, K), BF16),
        pltpu.VMEM((rows, V), BF16),
        pltpu.VMEM((8, 128), F32),
        pltpu.VMEM((8, 128), F32),
        pltpu.VMEM((8, K), F32),
        pltpu.VMEM((8, K), F32),
        pltpu.VMEM((V, K), BF16),
        pltpu.VMEM((half, K), BF16),
        pltpu.VMEM((half, K), BF16),
        pltpu.VMEM((half, K), BF16),
        pltpu.VMEM((half, K), BF16),
        pltpu.VMEM((V, K), BF16),
        pltpu.VMEM((2, rows, feats), BF16),
        pltpu.VMEM((2, rows, feats), BF16),
        pltpu.VMEM((rows, feats), BF16),
        pltpu.VMEM((rows, feats), BF16),
        pltpu.VMEM((rows, feats), F32),
        pltpu.VMEM((rows, feats), F32),
        dma((8,)),
        dma,
        dma((TOKEN_CHUNKS,)), dma((TOKEN_CHUNKS,)),
        dma((TOKEN_CHUNKS,)), dma((TOKEN_CHUNKS,)),
        dma((TOKEN_CHUNKS,)), dma((TOKEN_CHUNKS,)),
        dma((2,)), dma((2,)),
        dma((STATE_CHUNKS,)), dma((STATE_CHUNKS,)),
        dma((STATE_CHUNKS,)), dma((STATE_CHUNKS,)),
        dma((STATE_CHUNKS,)), dma((STATE_CHUNKS,)),
        dma((2, OUT_CHUNKS)), dma((2, OUT_CHUNKS)),
        dma((OUT_CHUNKS,)), dma((OUT_CHUNKS,)),
        dma((3,)), dma((3,)),
    ]
    return pl.pallas_call(
        functools.partial(kernel, pairs),
        out_shape=jax.ShapeDtypeStruct((rows, feats), BF16),
        in_specs=[hbm, vmem, hbm, hbm, hbm, hbm, vmem, vmem, vmem, vmem, hbm, vmem],
        out_specs=vmem,
        scratch_shapes=scratch,
        compiler_params=pltpu.CompilerParams(
            collective_id=0, has_side_effects=True, vmem_limit_bytes=62 * 2**20),
        cost_estimate=pl.CostEstimate(flops=2_500_000_000, bytes_accessed=10_000_000, transcendentals=400_000),
        name="gla",
    )(
        tokens,
        norm_gain.reshape(4, 1, feats),
        w_query.reshape(4, feats, K),
        w_key.reshape(4, feats, K),
        w_value.reshape(4, feats, V),
        w_gate_out.reshape(4, feats, V),
        gate_down.T,
        gate_up,
        gate_bias.reshape(1, K),
        head_gain.reshape(1, V),
        w_out,
        request_ids.reshape(1, rows),
    )


def solution(mesh):
    return jax.shard_map(
        functools.partial(per_device, mesh.shape["seq"] // 2),
        mesh=mesh,
        in_specs=(
            P("seq", "tp"),
            P(),
            P(None, "tp"),
            P(None, "tp"),
            P(None, "tp"),
            P(None, "tp"),
            P(),
            P(None, "tp"),
            P("tp"),
            P("tp"),
            P("tp", None),
            P("seq"),
        ),
        out_specs=P("seq", "tp"),
        check_vma=False,
    )
```

time: 188 us -> 43.3 us (0.23); the launches traced: 184 us -> 42.9 us
  waiting for transfers between devices: 91.8 us -> 0 us
  Pallas kernels: 0 us -> 41.2 us
  other arithmetic: 19.8 us -> 0 us
  matrix products: 18.1 us -> 0 us
  blocking collectives: 16.1 us -> 0 us
  between operations: 14.6 us -> 0.01 us
  local copies, waits for them, and re-layouts: 14.1 us -> 1.67 us
  loops' own time: 5.09 us -> 0 us
  starting transfers between devices: 4.79 us -> 0 us
    all_gather x2 -> x0, waiting for transfers between devices: 66 us -> none  [the longest x1 56.6 us: entering(): everything = jax.tree.map(lambda part: lax.all_gather(part, axis), shard)]
    pallas_call x0 -> x1, Pallas kernels: none -> 41.2 us  [per_device(): pl.pallas_call(functools.partial(kernel, pairs), out_shape=jax.ShapeDtype...]
    reduce_scatter x1 -> x0, waiting for transfers between devices: 24.1 us -> none  [per_device(): lax.psum_scatter(partial_out.astype(jnp.bfloat16), 'tp', scatter_dimensio...]
    dot_general x15 -> x0, matrix products: 18.1 us -> none  [the longest x4 3.76 us: group_terms(): intra = jnp.dot(weights, value, preferred_element_type=jnp.float32)]
    all_gather x1 -> x0, blocking collectives: 16.1 us -> none  [entering(): everything = jax.tree.map(lambda part: lax.all_gather(part, axis), shard)]
    select_n x8 -> x0, other arithmetic: 9.43 us -> none  [turn(): return jax.tree.map(lambda a, b: jnp.where(reached, a, b), new, before)]
    dynamic_update_slice x8 -> x0, other arithmetic: 5.9 us -> none  [local_pass(): lax.scan(step, start, (query, key, value, log_decay_rate, request_id_block))]
    dynamic_update_slice x8 -> x0, local copies, waits for them, and re-layouts: 5.34 us -> none  [local_pass(): lax.scan(step, start, (query, key, value, log_decay_rate, request_id_block))]
  transfers between devices with their start and end apart: 4 -> 0, of which waited for: 4 -> 0; matrix products, arithmetic and copies ran while one was open for 1% -> 0% of each run, Pallas kernels for 0% -> 0%
where the time goes in v1:
time: 43.3 us; the launch traced here: 42.9 us
  Pallas kernels  41.2 us (95%)
  local copies, waits for them, and re-layouts  1.67 us (4%)
    pallas_call x1, Pallas kernels, per_device(): pl.pallas_call(functools.partial(kernel, pairs), out_shape=jax.ShapeDtype...  41.2 us
    unnamed x1, local copies, waits for them, and re-layouts  1.67 us

profile of v1, /device:TPU:26, one launch (start us, length us, event | category | flops | bytes accessed | tf_op | source)
XLA Modules:
  0.0 42.9 jit_solution(16572732527021763767)
XLA Ops:
  0.0 41.2 %gla.1 = bf16[256,512]{1,0:T(8,128)(2,1)} custom-call(bf16[256,512]{1,0:T(8,128)(2,1)} %tokens_ref.1, f32[4,1,512]{2,1,0:T(1,128)} %bitcast.14, bf16[4,512,256]{2,1,0:T(8,128)(2,1)} %bitcast.11, bf16[4,512,256]{2,1,0:T(8,128)(2,1)} %bitcast.12, bf16[4,512,512]{2,1,0:T(8,128)(2,1)} %bitcast.9, bf16[4,512,512]{2,1,0:T(8,128)(2,1)} %bitcast.10, ...), custom_call_target="tpu_custom_call" | custom-call | flops 2500000000 | bytes 10000000 | tf_op jit(solution)/shard_map/gla/pallas_call | solution.py:366
  41.2 1.7 %copy.14 = bf16[256,512]{1,0:T(8,128)(2,1)} copy(bf16[256,512]{1,0:T(8,128)(2,1)} %gla.1) | data formatting | bytes 524288

commit v2 on v1

--- a/solution.py
+++ b/solution.py
@@ -15,7 +15,7 @@
 MESH = pl.DeviceIdType.MESH
 TOKEN_CHUNKS = 4
 STATE_CHUNKS = 4
-OUT_CHUNKS = 2
+OUT_CHUNKS = 4
 
 
 def dot(a, b):
@@ -40,7 +40,7 @@
     attn_ref, qin_ref, gated_ref,
     id_out, id_in, p_own, p_other,
     s_own, s_other, e_in, e_out, i_out, incoming,
-    mate_out, mate_in, x_out, x_in, keep_x, keep_own,
+    mate_out, mate_in, x_out, x_in, keep_x, keep_own, pair_first, pair_state,
     load_sem, tok_sem, tok_x, tok_x_in, tok_mate, tok_mate_in, tok_fwd, tok_fwd_in,
     id_sem, p_sem, s_sem, s_sem_in, e_sem, e_sem_in, i_sem, i_sem_in,
     m_sem, m_sem_in, x_sem, x_sem_in, ssq_sem, ssq_sem_in,
@@ -118,11 +118,17 @@
     def _():
         send_id.start()
 
-    def project(block):
-        xg = (tok[block].astype(F32) * r * gain_ref[block]).astype(BF16)
+    def normed(block):
+        return (tok[block].astype(F32) * r * gain_ref[block]).astype(BF16)
+
+    def project_state(block):
+        xg = normed(block)
         acc_low[...] += dot_nt(xg, down_ref[:, pl.ds(pl.multiple_of(block * feats, feats), feats)])
         acc_k[...] += dot(xg, wk[block])
         acc_v[...] += dot(xg, wv[block])
+
+    def project_read(block):
+        xg = normed(block)
         acc_q[...] += dot(xg, wq[block])
         acc_g[...] += dot(xg, wg[block])
 
@@ -133,19 +139,22 @@
     r = jnp.broadcast_to(scale_row, (128, rows)).T[:, 0:1]
     for load in loads[:4]:
         load.wait()
-    project(t)
+    project_state(t)
+    project_read(t)
     from_x[0].wait_recv()
     forward[0].start()
     for c in range(TOKEN_CHUNKS):
         from_mate[c].wait_recv()
-    project(mate)
+    project_state(mate)
+    project_read(mate)
     for c in range(1, TOKEN_CHUNKS):
         from_x[c].wait_recv()
         forward[c].start()
-    project(across)
+    project_state(across)
+    project_read(across)
     for c in range(TOKEN_CHUNKS):
         from_fwd[c].wait_recv()
-    project(diagonal)
+    project_state(diagonal)
 
     low = acc_low[...].astype(BF16)
     z = dot(low, up_ref[...]) + bias_ref[...]
@@ -204,6 +213,7 @@
     give = [remote(small(i_out, c), part(incoming, y, c), i_sem.at[c], i_sem_in.at[c], (partner, t)) for c in range(STATE_CHUNKS)]
     take = [remote(small(i_out, c), part(incoming, 1 - y, c), i_sem.at[c], i_sem_in.at[c], (partner, t)) for c in range(STATE_CHUNKS)]
 
+    project_read(diagonal)
     grow = jnp.exp(cum)
     query = acc_q[...].astype(BF16).astype(F32)
     qdec = (query * grow * K ** -0.5).astype(BF16)
@@ -233,38 +243,44 @@
     own_decay, other_decay = p_own[0:1, :], p_other[0:1, :]
     p0 = own_decay * first + other_decay * second
     p1 = own_decay * second + other_decay * first
+    both = p0 * p1
+
+    def place(c):
+        return pl.ds(pl.multiple_of(y * half + c * span, span), span)
+
     for c in range(STATE_CHUNKS):
         swap[c].wait_recv()
         mine = pl.ds(c * span, span)
-        place = pl.ds(pl.multiple_of(y * half + c * span, span), span)
-        a, b = s_own[place, :].astype(F32), s_other[mine, :].astype(F32)
+        a, b = s_own[place(c), :].astype(F32), s_other[mine, :].astype(F32)
         s0 = a * first + b * second
         s1 = a * second + b * first
+        pair_first[mine, :] = s0
+        pair_state[mine, :] = p1 * s0 + s1
+
+    for c in range(STATE_CHUNKS):
+        mine = pl.ds(c * span, span)
 
         @pl.when(g > 0)
         def _():
             chain[c].wait_recv()
 
-        entry = e_in[mine, :].astype(F32)
-        middle_state = p0 * entry + s0
-        e_out[mine, :] = (p1 * middle_state + s1).astype(BF16)
-
         @pl.when(g < last)
         def _():
+            e_out[mine, :] = (both * e_in[mine, :].astype(F32) + pair_state[mine, :]).astype(BF16)
             chain[c].start()
 
+        entry = e_in[mine, :].astype(F32)
+        middle_state = p0 * entry + pair_first[mine, :]
         i_out[mine, :] = (middle_state * first + entry * second).astype(BF16)
         give[c].start()
-        incoming[place, :] = (entry * first + middle_state * second).astype(BF16)
+        incoming[place(c), :] = (entry * first + middle_state * second).astype(BF16)
+    opengate = acc_g[...]
+    acc_g[...] = head_gain_ref[...] * (opengate * jax.nn.sigmoid(opengate))
+    for load in loads[4:]:
+        load.wait()
     for c in range(STATE_CHUNKS):
         take[c].wait_recv()
 
-    attn = attn_ref[...] + dot_nt(qin_ref[...], incoming[...])
-    scale = lax.rsqrt(jnp.mean(attn * attn, axis=-1, keepdims=True) + 1e-5)
-    opengate = acc_g[...]
-    gated_ref[...] = (attn * scale * head_gain_ref[...] * (opengate * jax.nn.sigmoid(opengate))).astype(BF16)
-    for load in loads[4:]:
-        load.wait()
     lot = rows // OUT_CHUNKS
 
     def lines(c):
@@ -276,6 +292,9 @@
     ]
     over = [remote(x_out.at[lines(c)], x_in.at[lines(c)], x_sem.at[c], x_sem_in.at[c], (s, across)) for c in range(OUT_CHUNKS)]
     for c in range(OUT_CHUNKS):
+        attn = attn_ref[lines(c), :] + dot_nt(qin_ref[lines(c), :], incoming[...])
+        scale = lax.rsqrt(jnp.mean(attn * attn, axis=-1, keepdims=True) + 1e-5)
+        gated_ref[lines(c), :] = (attn * scale * acc_g[lines(c), :]).astype(BF16)
         mate_out[0, lines(c), :] = dot(gated_ref[lines(c), :], wo[diagonal]).astype(BF16)
         share[0][c].start()
         keep_x[lines(c), :] = dot(gated_ref[lines(c), :], wo[across])
@@ -350,6 +369,8 @@
         pltpu.VMEM((rows, feats), BF16),
         pltpu.VMEM((rows, feats), F32),
         pltpu.VMEM((rows, feats), F32),
+        pltpu.VMEM((half, K), F32),
+        pltpu.VMEM((half, K), F32),
         dma((8,)),
         dma,
         dma((TOKEN_CHUNKS,)), dma((TOKEN_CHUNKS,)),

time: 43.3 us -> 44.7 us (1.032)
  Pallas kernels: 41.2 us -> 42.9 us
    pallas_call x1, Pallas kernels: 41.2 us -> 42.9 us  [per_device(): pl.pallas_call(functools.partial(kernel, pairs), out_shape=jax.ShapeDtype...]
where the time goes in v2:
time: 44.7 us; the launch traced here: 44.5 us
  Pallas kernels  42.9 us (96%)
  local copies, waits for them, and re-layouts  1.67 us (4%)
    pallas_call x1, Pallas kernels, per_device(): pl.pallas_call(functools.partial(kernel, pairs), out_shape=jax.ShapeDtype...  42.9 us
    unnamed x1, local copies, waits for them, and re-layouts  1.67 us

profile of v2, /device:TPU:26, one launch (start us, length us, event | category | flops | bytes accessed | tf_op | source)
XLA Modules:
  0.0 44.5 jit_solution(5665298403607167583)
XLA Ops:
  0.0 42.9 %gla.1 = bf16[256,512]{1,0:T(8,128)(2,1)} custom-call(bf16[256,512]{1,0:T(8,128)(2,1)} %tokens_ref.1, f32[4,1,512]{2,1,0:T(1,128)} %bitcast.14, bf16[4,512,256]{2,1,0:T(8,128)(2,1)} %bitcast.11, bf16[4,512,256]{2,1,0:T(8,128)(2,1)} %bitcast.12, bf16[4,512,512]{2,1,0:T(8,128)(2,1)} %bitcast.9, bf16[4,512,512]{2,1,0:T(8,128)(2,1)} %bitcast.10, ...), custom_call_target="tpu_custom_call" | custom-call | flops 2500000000 | bytes 10000000 | tf_op jit(solution)/shard_map/gla/pallas_call | solution.py:387
  42.9 1.7 %copy.14 = bf16[256,512]{1,0:T(8,128)(2,1)} copy(bf16[256,512]{1,0:T(8,128)(2,1)} %gla.1) | data formatting | bytes 524288

commit v3 on v2

--- a/solution.py
+++ b/solution.py
@@ -15,7 +15,7 @@
 MESH = pl.DeviceIdType.MESH
 TOKEN_CHUNKS = 4
 STATE_CHUNKS = 4
-OUT_CHUNKS = 4
+OUT_CHUNKS = 2
 
 
 def dot(a, b):
@@ -40,7 +40,7 @@
     attn_ref, qin_ref, gated_ref,
     id_out, id_in, p_own, p_other,
     s_own, s_other, e_in, e_out, i_out, incoming,
-    mate_out, mate_in, x_out, x_in, keep_x, keep_own, pair_first, pair_state,
+    mate_out, mate_in, x_out, x_in, keep_x, keep_own, pair_first,
     load_sem, tok_sem, tok_x, tok_x_in, tok_mate, tok_mate_in, tok_fwd, tok_fwd_in,
     id_sem, p_sem, s_sem, s_sem_in, e_sem, e_sem_in, i_sem, i_sem_in,
     m_sem, m_sem_in, x_sem, x_sem_in, ssq_sem, ssq_sem_in,
@@ -209,7 +209,11 @@
     swap = [remote(part(s_own, 1 - y, c), small(s_other, c), s_sem.at[c], s_sem_in.at[c], (partner, t)) for c in range(STATE_CHUNKS)]
     for c in range(STATE_CHUNKS):
         swap[c].start()
-    chain = [remote(small(e_out, c), small(e_in, c), e_sem.at[c], e_sem_in.at[c], (s + 2, t)) for c in range(STATE_CHUNKS)]
+    reach = pairs // 2
+    chain = [
+        [remote(small(e_out.at[k], c), small(e_in.at[k], c), e_sem.at[k, c], e_sem_in.at[k, c], (s + 2, t)) for c in range(STATE_CHUNKS)]
+        for k in range(reach)
+    ]
     give = [remote(small(i_out, c), part(incoming, y, c), i_sem.at[c], i_sem_in.at[c], (partner, t)) for c in range(STATE_CHUNKS)]
     take = [remote(small(i_out, c), part(incoming, 1 - y, c), i_sem.at[c], i_sem_in.at[c], (partner, t)) for c in range(STATE_CHUNKS)]
 
@@ -233,9 +237,10 @@
             qdec[mine].astype(F32) * jnp.exp(sum(totals[:b], zero)) * from_prev[mine]
         ).astype(BF16)
 
-    @pl.when(g == 0)
-    def _():
-        e_in[...] = jnp.zeros_like(e_in)
+    for k in range(reach):
+        @pl.when(g <= k)
+        def _():
+            e_in[k] = jnp.zeros_like(e_in[k])
 
     second = y.astype(F32)
     first = 1.0 - second
@@ -255,21 +260,35 @@
         s0 = a * first + b * second
         s1 = a * second + b * first
         pair_first[mine, :] = s0
-        pair_state[mine, :] = p1 * s0 + s1
+
+        @pl.when(g < last)
+        def _():
+            e_out[0, mine, :] = (p1 * s0 + s1).astype(BF16)
+            chain[0][c].start()
+
+    for k in range(1, reach):
+        for c in range(STATE_CHUNKS):
+            mine = pl.ds(c * span, span)
+
+            @pl.when(g >= k)
+            def _():
+                chain[k - 1][c].wait_recv()
+
+            @pl.when((g >= k) & (g < last))
+            def _():
+                e_out[k, mine, :] = (both * e_in[k - 1, mine, :].astype(F32)).astype(BF16)
+                chain[k][c].start()
 
     for c in range(STATE_CHUNKS):
         mine = pl.ds(c * span, span)
 
-        @pl.when(g > 0)
+        @pl.when(g >= reach)
         def _():
-            chain[c].wait_recv()
-
-        @pl.when(g < last)
-        def _():
-            e_out[mine, :] = (both * e_in[mine, :].astype(F32) + pair_state[mine, :]).astype(BF16)
-            chain[c].start()
-
-        entry = e_in[mine, :].astype(F32)
+            chain[reach - 1][c].wait_recv()
+
+        entry = e_in[0, mine, :].astype(F32)
+        for k in range(1, reach):
+            entry += e_in[k, mine, :].astype(F32)
         middle_state = p0 * entry + pair_first[mine, :]
         i_out[mine, :] = (middle_state * first + entry * second).astype(BF16)
         give[c].start()
@@ -291,8 +310,9 @@
         for k in range(2)
     ]
     over = [remote(x_out.at[lines(c)], x_in.at[lines(c)], x_sem.at[c], x_sem_in.at[c], (s, across)) for c in range(OUT_CHUNKS)]
+    attn_ref[...] += dot_nt(qin_ref[...], incoming[...])
     for c in range(OUT_CHUNKS):
-        attn = attn_ref[lines(c), :] + dot_nt(qin_ref[lines(c), :], incoming[...])
+        attn = attn_ref[lines(c), :]
         scale = lax.rsqrt(jnp.mean(attn * attn, axis=-1, keepdims=True) + 1e-5)
         gated_ref[lines(c), :] = (attn * scale * acc_g[lines(c), :]).astype(BF16)
         mate_out[0, lines(c), :] = dot(gated_ref[lines(c), :], wo[diagonal]).astype(BF16)
@@ -320,10 +340,11 @@
     def _():
         send_id.wait_send()
 
-    @pl.when(g < last)
-    def _():
-        for c in range(STATE_CHUNKS):
-            chain[c].wait_send()
+    for k in range(reach):
+        @pl.when((g >= k) & (g < last))
+        def _():
+            for c in range(STATE_CHUNKS):
+                chain[k][c].wait_send()
 
 
 def per_device(
@@ -359,8 +380,8 @@
         pltpu.VMEM((8, K), F32),
         pltpu.VMEM((V, K), BF16),
         pltpu.VMEM((half, K), BF16),
-        pltpu.VMEM((half, K), BF16),
-        pltpu.VMEM((half, K), BF16),
+        pltpu.VMEM((pairs // 2, half, K), BF16),
+        pltpu.VMEM((pairs // 2, half, K), BF16),
         pltpu.VMEM((half, K), BF16),
         pltpu.VMEM((V, K), BF16),
         pltpu.VMEM((2, rows, feats), BF16),
@@ -370,7 +391,6 @@
         pltpu.VMEM((rows, feats), F32),
         pltpu.VMEM((rows, feats), F32),
         pltpu.VMEM((half, K), F32),
-        pltpu.VMEM((half, K), F32),
         dma((8,)),
         dma,
         dma((TOKEN_CHUNKS,)), dma((TOKEN_CHUNKS,)),
@@ -378,7 +398,7 @@
         dma((TOKEN_CHUNKS,)), dma((TOKEN_CHUNKS,)),
         dma((2,)), dma((2,)),
         dma((STATE_CHUNKS,)), dma((STATE_CHUNKS,)),
-        dma((STATE_CHUNKS,)), dma((STATE_CHUNKS,)),
+        dma((pairs // 2, STATE_CHUNKS)), dma((pairs // 2, STATE_CHUNKS)),
         dma((STATE_CHUNKS,)), dma((STATE_CHUNKS,)),
         dma((2, OUT_CHUNKS)), dma((2, OUT_CHUNKS)),
         dma((OUT_CHUNKS,)), dma((OUT_CHUNKS,)),

time: 44.7 us -> 40.7 us (0.911); the launches traced: 44.5 us -> 40 us
  Pallas kernels: 42.9 us -> 38.3 us
    pallas_call x1, Pallas kernels: 42.9 us -> 38.3 us  [per_device(): pl.pallas_call(functools.partial(kernel, pairs), out_shape=jax.ShapeDtype...]
where the time goes in v3:
time: 40.7 us; the launch traced here: 40 us
  Pallas kernels  38.3 us (94%)
  local copies, waits for them, and re-layouts  1.67 us (4%)
    pallas_call x1, Pallas kernels, per_device(): pl.pallas_call(functools.partial(kernel, pairs), out_shape=jax.ShapeDtype...  38.3 us
    unnamed x1, local copies, waits for them, and re-layouts  1.67 us

profile of v3, /device:TPU:26, one launch (start us, length us, event | category | flops | bytes accessed | tf_op | source)
XLA Modules:
  0.0 40.0 jit_solution(10054716366731479864)
XLA Ops:
  0.0 38.3 %gla.1 = bf16[256,512]{1,0:T(8,128)(2,1)} custom-call(bf16[256,512]{1,0:T(8,128)(2,1)} %tokens_ref.1, f32[4,1,512]{2,1,0:T(1,128)} %bitcast.14, bf16[4,512,256]{2,1,0:T(8,128)(2,1)} %bitcast.11, bf16[4,512,256]{2,1,0:T(8,128)(2,1)} %bitcast.12, bf16[4,512,512]{2,1,0:T(8,128)(2,1)} %bitcast.9, bf16[4,512,512]{2,1,0:T(8,128)(2,1)} %bitcast.10, ...), custom_call_target="tpu_custom_call" | custom-call | flops 2500000000 | bytes 10000000 | tf_op jit(solution)/shard_map/gla/pallas_call | solution.py:407
  38.3 1.7 %copy.14 = bf16[256,512]{1,0:T(8,128)(2,1)} copy(bf16[256,512]{1,0:T(8,128)(2,1)} %gla.1) | data formatting | bytes 524288

commit v4 on v3

--- a/solution.py
+++ b/solution.py
@@ -40,7 +40,7 @@
     attn_ref, qin_ref, gated_ref,
     id_out, id_in, p_own, p_other,
     s_own, s_other, e_in, e_out, i_out, incoming,
-    mate_out, mate_in, x_out, x_in, keep_x, keep_own, pair_first,
+    mate_out, mate_in, x_out, x_in, keep_own, pair_first,
     load_sem, tok_sem, tok_x, tok_x_in, tok_mate, tok_mate_in, tok_fwd, tok_fwd_in,
     id_sem, p_sem, s_sem, s_sem_in, e_sem, e_sem_in, i_sem, i_sem_in,
     m_sem, m_sem_in, x_sem, x_sem_in, ssq_sem, ssq_sem_in,
@@ -223,7 +223,8 @@
     qdec = (query * grow * K ** -0.5).astype(BF16)
     kinv = (key * jnp.exp(-cum)).astype(BF16)
     from_prev = jnp.where(id_col[:, 0:1] == id_prev, 1.0, 0.0)
-    for b in range(blocks):
+
+    def local_block(b):
         mine = slice(b * C, (b + 1) * C)
         seen = (b + 1) * C
         keys = [
@@ -266,6 +267,8 @@
             e_out[0, mine, :] = (p1 * s0 + s1).astype(BF16)
             chain[0][c].start()
 
+    local_block(0)
+    local_block(1)
     for k in range(1, reach):
         for c in range(STATE_CHUNKS):
             mine = pl.ds(c * span, span)
@@ -279,6 +282,7 @@
                 e_out[k, mine, :] = (both * e_in[k - 1, mine, :].astype(F32)).astype(BF16)
                 chain[k][c].start()
 
+    local_block(2)
     for c in range(STATE_CHUNKS):
         mine = pl.ds(c * span, span)
 
@@ -293,6 +297,8 @@
         i_out[mine, :] = (middle_state * first + entry * second).astype(BF16)
         give[c].start()
         incoming[place(c), :] = (entry * first + middle_state * second).astype(BF16)
+    for b in range(3, blocks):
+        local_block(b)
     opengate = acc_g[...]
     acc_g[...] = head_gain_ref[...] * (opengate * jax.nn.sigmoid(opengate))
     for load in loads[4:]:
@@ -317,10 +323,10 @@
         gated_ref[lines(c), :] = (attn * scale * acc_g[lines(c), :]).astype(BF16)
         mate_out[0, lines(c), :] = dot(gated_ref[lines(c), :], wo[diagonal]).astype(BF16)
         share[0][c].start()
-        keep_x[lines(c), :] = dot(gated_ref[lines(c), :], wo[across])
     for c in range(OUT_CHUNKS):
+        keep_x = dot(gated_ref[lines(c), :], wo[across])
         share[0][c].wait_recv()
-        x_out[lines(c), :] = (keep_x[lines(c), :] + mate_in[0, lines(c), :].astype(F32)).astype(BF16)
+        x_out[lines(c), :] = (keep_x + mate_in[0, lines(c), :].astype(F32)).astype(BF16)
         over[c].start()
     for c in range(OUT_CHUNKS):
         mate_out[1, lines(c), :] = dot(gated_ref[lines(c), :], wo[mate]).astype(BF16)
@@ -389,7 +395,6 @@
         pltpu.VMEM((rows, feats), BF16),
         pltpu.VMEM((rows, feats), BF16),
         pltpu.VMEM((rows, feats), F32),
-        pltpu.VMEM((rows, feats), F32),
         pltpu.VMEM((half, K), F32),
         dma((8,)),
         dma,

time: 40.7 us -> 40.6 us (level)
  no operation moved by 1% of the time
where the time goes in v4:
time: 40.6 us; the launch traced here: 39.9 us
  Pallas kernels  38.2 us (94%)
  local copies, waits for them, and re-layouts  1.67 us (4%)
    pallas_call x1, Pallas kernels, per_device(): pl.pallas_call(functools.partial(kernel, pairs), out_shape=jax.ShapeDtype...  38.2 us
    unnamed x1, local copies, waits for them, and re-layouts  1.67 us

profile of v4, /device:TPU:26, one launch (start us, length us, event | category | flops | bytes accessed | tf_op | source)
XLA Modules:
  0.0 39.9 jit_solution(14466168932843628166)
XLA Ops:
  0.0 38.2 %gla.1 = bf16[256,512]{1,0:T(8,128)(2,1)} custom-call(bf16[256,512]{1,0:T(8,128)(2,1)} %tokens_ref.1, f32[4,1,512]{2,1,0:T(1,128)} %bitcast.14, bf16[4,512,256]{2,1,0:T(8,128)(2,1)} %bitcast.11, bf16[4,512,256]{2,1,0:T(8,128)(2,1)} %bitcast.12, bf16[4,512,512]{2,1,0:T(8,128)(2,1)} %bitcast.9, bf16[4,512,512]{2,1,0:T(8,128)(2,1)} %bitcast.10, ...), custom_call_target="tpu_custom_call" | custom-call | flops 2500000000 | bytes 10000000 | tf_op jit(solution)/shard_map/gla/pallas_call | solution.py:412
  38.2 1.7 %copy.14 = bf16[256,512]{1,0:T(8,128)(2,1)} copy(bf16[256,512]{1,0:T(8,128)(2,1)} %gla.1) | data formatting | bytes 524288

commit v5 on v4

--- a/solution.py
+++ b/solution.py
@@ -126,9 +126,9 @@
         acc_low[...] += dot_nt(xg, down_ref[:, pl.ds(pl.multiple_of(block * feats, feats), feats)])
         acc_k[...] += dot(xg, wk[block])
         acc_v[...] += dot(xg, wv[block])
-
-    def project_read(block):
-        xg = normed(block)
+        return xg
+
+    def project_read(block, xg):
         acc_q[...] += dot(xg, wq[block])
         acc_g[...] += dot(xg, wg[block])
 
@@ -139,22 +139,19 @@
     r = jnp.broadcast_to(scale_row, (128, rows)).T[:, 0:1]
     for load in loads[:4]:
         load.wait()
-    project_state(t)
-    project_read(t)
+    project_read(t, project_state(t))
     from_x[0].wait_recv()
     forward[0].start()
     for c in range(TOKEN_CHUNKS):
         from_mate[c].wait_recv()
-    project_state(mate)
-    project_read(mate)
+    project_read(mate, project_state(mate))
     for c in range(1, TOKEN_CHUNKS):
         from_x[c].wait_recv()
         forward[c].start()
-    project_state(across)
-    project_read(across)
+    project_read(across, project_state(across))
     for c in range(TOKEN_CHUNKS):
         from_fwd[c].wait_recv()
-    project_state(diagonal)
+    last_normed = project_state(diagonal)
 
     low = acc_low[...].astype(BF16)
     z = dot(low, up_ref[...]) + bias_ref[...]
@@ -217,7 +214,7 @@
     give = [remote(small(i_out, c), part(incoming, y, c), i_sem.at[c], i_sem_in.at[c], (partner, t)) for c in range(STATE_CHUNKS)]
     take = [remote(small(i_out, c), part(incoming, 1 - y, c), i_sem.at[c], i_sem_in.at[c], (partner, t)) for c in range(STATE_CHUNKS)]
 
-    project_read(diagonal)
+    project_read(diagonal, last_normed)
     grow = jnp.exp(cum)
     query = acc_q[...].astype(BF16).astype(F32)
     qdec = (query * grow * K ** -0.5).astype(BF16)

time: 40.6 us -> 40.6 us (level)
  no operation moved by 1% of the time
where the time goes in v5:
time: 40.6 us; the launch traced here: 39.9 us
  Pallas kernels  38.2 us (94%)
  local copies, waits for them, and re-layouts  1.67 us (4%)
    pallas_call x1, Pallas kernels, per_device(): pl.pallas_call(functools.partial(kernel, pairs), out_shape=jax.ShapeDtype...  38.2 us
    unnamed x1, local copies, waits for them, and re-layouts  1.67 us

profile of v5, /device:TPU:26, one launch (start us, length us, event | category | flops | bytes accessed | tf_op | source)
XLA Modules:
  0.0 39.9 jit_solution(17453381134048035106)
XLA Ops:
  0.0 38.2 %gla.1 = bf16[256,512]{1,0:T(8,128)(2,1)} custom-call(bf16[256,512]{1,0:T(8,128)(2,1)} %tokens_ref.1, f32[4,1,512]{2,1,0:T(1,128)} %bitcast.14, bf16[4,512,256]{2,1,0:T(8,128)(2,1)} %bitcast.11, bf16[4,512,256]{2,1,0:T(8,128)(2,1)} %bitcast.12, bf16[4,512,512]{2,1,0:T(8,128)(2,1)} %bitcast.9, bf16[4,512,512]{2,1,0:T(8,128)(2,1)} %bitcast.10, ...), custom_call_target="tpu_custom_call" | custom-call | flops 2500000000 | bytes 10000000 | tf_op jit(solution)/shard_map/gla/pallas_call | solution.py:409
  38.2 1.7 %copy.14 = bf16[256,512]{1,0:T(8,128)(2,1)} copy(bf16[256,512]{1,0:T(8,128)(2,1)} %gla.1) | data formatting | bytes 524288

commit v6 on v5

--- a/solution.py
+++ b/solution.py
@@ -148,7 +148,7 @@
     for c in range(1, TOKEN_CHUNKS):
         from_x[c].wait_recv()
         forward[c].start()
-    project_read(across, project_state(across))
+    across_normed = project_state(across)
     for c in range(TOKEN_CHUNKS):
         from_fwd[c].wait_recv()
     last_normed = project_state(diagonal)
@@ -214,6 +214,7 @@
     give = [remote(small(i_out, c), part(incoming, y, c), i_sem.at[c], i_sem_in.at[c], (partner, t)) for c in range(STATE_CHUNKS)]
     take = [remote(small(i_out, c), part(incoming, 1 - y, c), i_sem.at[c], i_sem_in.at[c], (partner, t)) for c in range(STATE_CHUNKS)]
 
+    project_read(across, across_normed)
     project_read(diagonal, last_normed)
     grow = jnp.exp(cum)
     query = acc_q[...].astype(BF16).astype(F32)

time: 40.6 us -> 40.4 us (level)
  no operation moved by 1% of the time
where the time goes in v6:
time: 40.4 us; the launch traced here: 39.7 us
  Pallas kernels  38 us (94%)
  local copies, waits for them, and re-layouts  1.67 us (4%)
    pallas_call x1, Pallas kernels, per_device(): pl.pallas_call(functools.partial(kernel, pairs), out_shape=jax.ShapeDtype...  38 us
    unnamed x1, local copies, waits for them, and re-layouts  1.67 us

profile of v6, /device:TPU:26, one launch (start us, length us, event | category | flops | bytes accessed | tf_op | source)
XLA Modules:
  0.0 39.7 jit_solution(594680564730076117)
XLA Ops:
  0.0 38.0 %gla.1 = bf16[256,512]{1,0:T(8,128)(2,1)} custom-call(bf16[256,512]{1,0:T(8,128)(2,1)} %tokens_ref.1, f32[4,1,512]{2,1,0:T(1,128)} %bitcast.14, bf16[4,512,256]{2,1,0:T(8,128)(2,1)} %bitcast.11, bf16[4,512,256]{2,1,0:T(8,128)(2,1)} %bitcast.12, bf16[4,512,512]{2,1,0:T(8,128)(2,1)} %bitcast.9, bf16[4,512,512]{2,1,0:T(8,128)(2,1)} %bitcast.10, ...), custom_call_target="tpu_custom_call" | custom-call | flops 2500000000 | bytes 10000000 | tf_op jit(solution)/shard_map/gla/pallas_call | solution.py:410
  38.0 1.7 %copy.14 = bf16[256,512]{1,0:T(8,128)(2,1)} copy(bf16[256,512]{1,0:T(8,128)(2,1)} %gla.1) | data formatting | bytes 524288
